TPU v7x, 32 devices: a whole 2x2x4 slice. The times are simulated.
32 devices in a mesh: seq: 8 (over z, y), mp: 4 (over x, core).
Axes of the slice: x: 2, y: 2, z: 4, core: 2. Of those that a mesh axis runs over, the one named last changes fastest.
Arguments:
- latents: bfloat16 [16, 128, 256], P('seq'), may hold values from -6 to 6
- conv_w: bfloat16 [3, 3, 256, 256], P(None, None, None, 'mp'), may hold values from -0.125 to 0.125
- embed_w: bfloat16 [4, 256, 4096], P(None, 'mp', 'seq'), may hold values from -0.1875 to 0.1875
- text_emb: bfloat16 [1024, 4096], P('seq', 'mp'), may hold values from -6 to 6
- wqkv: bfloat16 [4096, 3, 2048], P(None, None, 'mp'), may hold values from -2 to 2
- seg_ids: int32 [1024], replicated, may hold values from 0 to 1, as said below
Outputs:
- attn: bfloat16 [1024, 2048], P('seq', 'mp')
Inputs may be any that keep to these rules, and one draw needn't show every extreme that they name: `seg_ids`: image n occupies one run of 512 positions that starts at a multiple of 64; runs come in the order of n and every image is present; 0 marks text.
All inputs are finite; a program needn't handle non-finite values.
Results may differ from a plain program's by a relative error of at most 0.015.
The roundings to bfloat16 on the way count: a program that leaves them out, or rounds other values in their place, can miss the bound.
Values may be sent and summed in bfloat16 or wider, within the bound.
A program may use at most 128 MiB of HBM per device.

v0:
```python
import jax
import jax.numpy as jnp
from jax import lax
from jax.sharding import PartitionSpec as P

HD = 128


def padded_2(cells, sides, width):
    for axis, dim in sides:
        count = lax.axis_size(axis)
        ends = count - 1
        head = lax.slice_in_dim(cells, 0, width, axis=dim)
        tail = lax.slice_in_dim(cells, cells.shape[dim] - width, cells.shape[dim], axis=dim)
        cells = jnp.concatenate(
            [
                lax.ppermute(tail, axis, [(i, (i + 1) % count) for i in range(ends)]),
                cells,
                lax.ppermute(head, axis, [((i + 1) % count, i) for i in range(ends)]),
            ],
            axis=dim,
        )
    return cells


def attend_block(carry, pieces, queries, query_pos, query_seg, seg_ids, scale):
    running, totals, outputs = carry
    key_blk, value_blk = pieces
    count = key_blk.shape[0]
    heads = queries.shape[1]
    head_size = queries.shape[2]
    key_heads = key_blk.reshape(count, heads, head_size)
    value_heads = value_blk.reshape(count, heads, head_size)
    key_pos = jnp.arange(count, dtype=jnp.int32)
    allowed = (key_pos[None, :] <= query_pos[:, None]) | (
        query_seg[:, None] == seg_ids[None, :]
    ) & (query_seg[:, None] > 0)
    scores = (
        jnp.einsum("qhd,khd->hqk", queries, key_heads, preferred_element_type=jnp.float32) * scale
    )
    scores = jnp.where(allowed[None], scores, -1e30)
    updated = jnp.maximum(running, jnp.max(scores, axis=-1))
    weights = jnp.where(allowed[None], jnp.exp(scores - updated[..., None]), 0.0)
    totals = jnp.sum(weights, axis=-1)
    probs = weights.astype(jnp.bfloat16)
    outputs = jnp.einsum("hqk,khd->hqd", probs, value_heads, preferred_element_type=jnp.float32)
    return (updated, totals, outputs)


def shards(latents, conv_w, embed_w, text_emb, wqkv, seg_ids):
    tile_rows = latents.shape[0]
    tile_cols = latents.shape[1]
    channels = latents.shape[2]
    chan_dev = conv_w.shape[3]
    patch_rows = tile_rows // 2
    patch_cols = tile_cols // 2
    seq_count = lax.axis_size("seq")
    image_rows = seq_count * patch_rows
    num_images = 1
    tok_rows = text_emb.shape[0]
    total_len = seg_ids.shape[0]
    seq_index = lax.axis_index("seq")
    mp_index = lax.axis_index("mp")
    extended = padded_2(latents, (("seq", 0),), 1)
    first_row = seq_index * tile_rows
    image_height = 2 * image_rows
    keep_top = first_row % image_height != 0
    keep_bottom = (first_row + tile_rows) % image_height != 0
    row_ids = jnp.arange(tile_rows + 2, dtype=jnp.int32)
    keep = jnp.where(row_ids == 0, keep_top, jnp.where(row_ids == tile_rows + 1, keep_bottom, True))
    extended = jnp.where(keep[:, None, None], extended, jnp.zeros_like(extended))
    padded = jnp.pad(extended, ((0, 0), (1, 1), (0, 0)))
    summed = jnp.zeros((tile_rows * tile_cols, chan_dev), jnp.float32)
    for row_step in range(3):
        for col_step in range(3):
            window = padded[
                row_step : row_step + tile_rows, col_step : col_step + tile_cols, :
            ].reshape(tile_rows * tile_cols, channels)
            summed = summed + jnp.dot(
                window, conv_w[row_step, col_step], preferred_element_type=jnp.float32
            )
    own_chan = lax.dynamic_slice_in_dim(latents, mp_index * chan_dev, chan_dev, 2)
    mixed = (
        own_chan.astype(jnp.float32) + jax.nn.silu(summed.reshape(tile_rows, tile_cols, chan_dev))
    ).astype(jnp.bfloat16)
    patches = (
        mixed.reshape(patch_rows, 2, patch_cols, 2, chan_dev)
        .transpose(0, 2, 1, 3, 4)
        .reshape(patch_rows * patch_cols, 4 * chan_dev)
    )
    positions = jnp.arange(total_len, dtype=jnp.int32)
    labels = jnp.arange(1, num_images + 1, dtype=jnp.int32)
    marks = seg_ids[None, :] == labels[:, None]
    starts = jnp.min(jnp.where(marks, positions[None, :], total_len), axis=1)
    base = seq_index * tok_rows
    my_pos = base + jnp.arange(tok_rows, dtype=jnp.int32)
    piece = lax.all_gather(patches, "seq", axis=0, tiled=True)
    count = piece.shape[0]
    token = jnp.arange(count, dtype=jnp.int32)
    row_glob = token // patch_cols
    column = token % patch_cols
    image = row_glob // image_rows
    inner = row_glob % image_rows
    begin = jnp.sum(jnp.where(image[:, None] == labels[None, :] - 1, starts[None, :], 0), axis=1)
    target = begin + inner * patch_cols + column
    select = (my_pos[:, None] == target[None, :]).astype(jnp.bfloat16)
    placed = jnp.dot(select, piece, preferred_element_type=jnp.float32).astype(jnp.bfloat16)
    piece = lax.all_gather(embed_w, "seq", axis=2, tiled=True)
    partial_emb = jnp.dot(
        placed, piece.reshape(4 * chan_dev, piece.shape[2]), preferred_element_type=jnp.float32
    )
    my_seg = lax.dynamic_slice_in_dim(seg_ids, base, tok_rows, 0)
    is_text = my_seg == 0
    feat_dev = text_emb.shape[1]
    text_part = jnp.where(is_text[:, None], text_emb.astype(jnp.float32), 0.0)
    own_cols = lax.dynamic_slice_in_dim(partial_emb, mp_index * feat_dev, feat_dev, 1)
    partial_emb = lax.dynamic_update_slice_in_dim(
        partial_emb, own_cols + text_part, mp_index * feat_dev, 1
    )
    hidden = lax.psum(partial_emb, "mp").astype(jnp.bfloat16)
    width = wqkv.shape[0]
    head_cols = wqkv.shape[2]
    head_size = HD
    heads_dev = head_cols // head_size
    qkv = jnp.dot(
        hidden, wqkv.reshape(width, 3 * head_cols), preferred_element_type=jnp.float32
    ).astype(jnp.bfloat16)
    qkv = qkv.reshape(tok_rows, 3, head_cols)
    queries = qkv[:, 0].reshape(tok_rows, heads_dev, head_size)
    key_rows = qkv[:, 1]
    value_rows = qkv[:, 2]
    scale = head_size ** (-0.5)
    fold_init = (
        jnp.full((heads_dev, tok_rows), -1e30, jnp.float32),
        jnp.zeros((heads_dev, tok_rows), jnp.float32),
        jnp.zeros((heads_dev, tok_rows, head_size), jnp.float32),
    )
    running, totals, outputs = attend_block(
        fold_init,
        (
            lax.all_gather(key_rows, "seq", axis=0, tiled=True),
            lax.all_gather(value_rows, "seq", axis=0, tiled=True),
        ),
        queries,
        my_pos,
        my_seg,
        seg_ids,
        scale,
    )
    result = outputs / totals[..., None]
    return result.transpose(1, 0, 2).reshape(tok_rows, heads_dev * head_size).astype(jnp.bfloat16)


def solution(mesh):
    return jax.shard_map(
        shards,
        mesh=mesh,
        in_specs=(
            P("seq", None, None),
            P(None, None, None, "mp"),
            P(None, "mp", "seq"),
            P("seq", "mp"),
            P(None, None, "mp"),
            P(),
        ),
        out_specs=P("seq", "mp"),
        check_vma=False,
    )
```

profile of v0, /device:TPU:0, one launch (start us, length us, event | category | flops | bytes accessed | tf_op | source)
XLA Modules:
  0.0 211.9 jit_solution(16861594560382529581)
XLA Ops:
  6.5 0.9 fusion.65
  7.4 4.9 %collective-permute-start = (bf16[1,128,256]{2,1,0:T(8,128)(2,1)S(1)}, bf16[1,128,256]{2,1,0:T(8,128)(2,1)S(1)}, u32[]{:S(2)}, u32[]{:S(2)}) collective-permute-start(bf16[1,128,256]{2,1,0:T(8,128)(2,1)S(1)} %get-tuple-element.19), channel_id=1, source_target_pairs={{0,4},{4,8},{8,12},{12,16},{16,20},{20,24},{24,28},{1,5},{5,9},{9,... | collective-permute-start | bytes 196616 | tf_op jit(solution)/shard_map/ppermute | solution.py:17
  12.3 1.3 collective-permute-start.1
  13.7 0.9 constant_dynamic-slice_fusion
  14.8 17.0 %copy.31 = bf16[4096,3,512]{0,2,1:T(8,128)(2,1)} copy(bf16[4096,3,512]{2,0,1:T(8,128)(2,1)} %param.10) | data formatting | bytes 25165824 | tf_op args[4]
  31.9 0.6 select_reduce_fusion
  32.5 0.7 fusion.52
  33.6 0.2 convolution_add_fusion.7
  33.8 0.2 convolution_add_fusion.6
  34.4 0.2 convolution_add_fusion.3
  35.5 34.2 %all_gather.12 = bf16[512,256]{1,0:T(8,128)(2,1)S(1)} all-gather(bf16[64,256]{1,0:T(8,128)(2,1)S(1)} %reshape.204), channel_id=1, replica_groups=mesh['seq'=8,'mp'=4] {'seq'}, dimensions={0}, use_global_device_ids=true | all-gather | bytes 294912 | tf_op jit(solution)/shard_map/all_gather | solution.py:97
  69.9 2.3 %fusion.6 = f32[128,4096]{1,0:T(8,128)S(1)} fusion(bf16[256,4096]{1,0:T(8,128)(2,1)} %bitcast.87, bf16[512,256]{1,0:T(8,128)(2,1)S(1)} %all_gather.12, s32[512]{0:T(512)S(1)} %fusion.52, s32[128]{0:T(128)S(1)} %iota_add_fusion), kind=kOutput, calls=%fused_computation.19 | convolution fusion | flops 302088192 | bytes 4459008 | tf_op jit(solution)/shard_map/dot_general | solution.py:109
  72.3 40.6 %all-reduce.2 = bf16[128,4096]{1,0:T(8,128)(2,1)S(1)} all-reduce(f32[128,4096]{1,0:T(8,128)S(1)} %add_dynamic-update-slice_fusion), channel_id=1, replica_groups=mesh['seq'=8,'mp'=4] {'mp'}, use_global_device_ids=true, to_apply=%region_1.2 | all-reduce | flops 524288 | bytes 3145728 | tf_op jit(solution)/shard_map/psum | solution.py:120
  113.0 8.8 %convolution_convert_fusion = bf16[128,1536]{1,0:T(8,128)(2,1)S(1)} fusion(bf16[4096,1536]{0,1:T(8,128)(2,1)} %bitcast.86, bf16[128,4096]{1,0:T(8,128)(2,1)S(1)} %all-reduce.2), kind=kOutput, calls=%fused_computation | convolution fusion | flops 1610809344 | bytes 14024704 | tf_op jit(solution)/shard_map/dot_general | solution.py:125
  121.8 0.2 copy.32
  122.0 0.7 fusion.64
  122.8 0.7 all-gather.10.cloned.1.call-update
  123.5 0.2 fusion.14
  123.7 38.3 %all-gather.8.cloned.1.call-done = bf16[1024,1,512]{0,2,1:T(8,128)(2,1)} async-done(((bf16[128,1,512]{0,2,1:T(8,128)(2,1)}), bf16[1024,1,512]{0,2,1:T(8,128)(2,1)}) %all-gather.8.cloned.1.call-update) | async-done | bytes 1048592 | tf_op jit(solution)/shard_map/all_gather | solution.py:141
  162.0 1.9 fusion
  163.9 0.7 fusion.1
  164.6 37.9 %all-gather.10.cloned.1.call-done = bf16[1024,1,512]{0,2,1:T(8,128)(2,1)} async-done(((bf16[128,1,512]{0,2,1:T(8,128)(2,1)}), bf16[1024,1,512]{0,2,1:T(8,128)(2,1)}) %all-gather.10.cloned.1.call-update) | async-done | bytes 1048592 | tf_op jit(solution)/shard_map/all_gather | solution.py:142
  202.5 2.0 fusion.4
  204.6 0.8 copy.35
  (35 shorter events, 2.3 us)
Async XLA Ops:
  6.5 63.3 %all-gather.6.cloned.1.call-start = ((), (), s32[]{:S(2)}) async-start(), calls=%async_computation | async-start | bytes 2359296 | tf_op jit(solution)/shard_map/all_gather | solution.py:108
  7.4 25.8 %collective-permute-start = (bf16[1,128,256]{2,1,0:T(8,128)(2,1)S(1)}, bf16[1,128,256]{2,1,0:T(8,128)(2,1)S(1)}, u32[]{:S(2)}, u32[]{:S(2)}) collective-permute-start(bf16[1,128,256]{2,1,0:T(8,128)(2,1)S(1)} %get-tuple-element.19), channel_id=1, source_target_pairs={{0,4},{4,8},{8,12},{12,16},{16,20},{20,24},{24,28},{1,5},{5,9},{9,... | collective-permute-start | bytes 196616 | tf_op jit(solution)/shard_map/ppermute | solution.py:17
  12.3 20.9 %collective-permute-start.1 = (bf16[1,128,256]{2,1,0:T(8,128)(2,1)S(1)}, bf16[1,128,256]{2,1,0:T(8,128)(2,1)S(1)}, u32[]{:S(2)}, u32[]{:S(2)}) collective-permute-start(bf16[1,128,256]{2,1,0:T(8,128)(2,1)S(1)} %get-tuple-element.20), channel_id=1, source_target_pairs={{4,0},{8,4},{12,8},{16,12},{20,16},{24,20},{28,24},{5,1},{9,5},{13... | collective-permute-start | bytes 196616 | tf_op jit(solution)/shard_map/ppermute | solution.py:19
  13.6 148.4 %all-gather.8.cloned.1.call-start = ((), (), s32[]{:S(2)}) async-start(), calls=%async_computation.1 | async-start | bytes 1179648 | tf_op jit(solution)/shard_map/all_gather | solution.py:141
  14.7 17.0 %copy-start.3 = (s32[1024]{0:T(1024)S(1)}, s32[1024]{0:T(1024)}, u32[]{:S(2)}) copy-start(s32[1024]{0:T(1024)} %param.11) | copy-start | bytes 12292
  14.8 18.5 %copy-start = (bf16[2,128,256]{2,1,0:T(8,128)(2,1)S(1)}, bf16[2,128,256]{2,1,0:T(8,128)(2,1)}, u32[]{:S(2)}) copy-start(bf16[2,128,256]{2,1,0:T(8,128)(2,1)} %param.6) | copy-start | bytes 393220
  31.8 1.7 copy-start.1
  69.9 2.3 %copy-start.2 = (bf16[128,1024]{1,0:T(8,128)(2,1)S(1)}, bf16[128,1024]{1,0:T(8,128)(2,1)}, u32[]{:S(2)}) copy-start(bf16[128,1024]{1,0:T(8,128)(2,1)} %param.9) | copy-start | bytes 786436
  122.8 79.8 %all-gather.10.cloned.1.call-start = ((), (), s32[]{:S(2)}) async-start(), calls=%async_computation.2 | async-start | bytes 1179648 | tf_op jit(solution)/shard_map/all_gather | solution.py:142
Sparse Core Ops, SparseCore 0:
  13.7 56.0 all-gather.5
  122.9 39.0 all-gather.7
  164.1 38.4 all-gather.9
where the time goes:
time: 213 us; the launch traced here: 212 us
  waiting for transfers between devices  77.1 us (36%)
  blocking collectives  74.8 us (35%)
  local copies, waits for them, and re-layouts  21.1 us (10%)
  matrix products  16.7 us (8%)
  between operations  13.3 us (6%)
  starting transfers between devices  6.25 us (3%)
  other arithmetic  2.6 us (1%)
    psum x1, blocking collectives, shards(): hidden = lax.psum(partial_emb, 'mp').astype(jnp.bfloat16)  40.6 us
    all_gather x1, waiting for transfers between devices, shards(): lax.all_gather(key_rows, 'seq', axis=0, tiled=True)  38.3 us
    all_gather x1, waiting for transfers between devices, shards(): lax.all_gather(value_rows, 'seq', axis=0, tiled=True)  37.9 us
    all_gather x1, blocking collectives, shards(): piece = lax.all_gather(patches, 'seq', axis=0, tiled=True)  34.2 us
    unnamed x10, local copies, waits for them, and re-layouts  17.1 us
    dot_general x1, matrix products, shards(): jnp.dot(hidden, wqkv.reshape(width, 3 * head_cols), preferred_element_typ...  8.83 us
    ppermute x1, starting transfers between devices, padded_2(): lax.ppermute(tail, axis, [(i, (i + 1) % count) for i in range(ends)])  4.87 us
  transfers between devices with their start and end apart: 5, of which 3 were waited for; matrix products, arithmetic and copies ran while one was open for 12% of the time, Pallas kernels for 0%

commit v1 on v0

--- a/solution.py
+++ b/solution.py
@@ -1,6 +1,10 @@
+import functools
+
 import jax
 import jax.numpy as jnp
 from jax import lax
+from jax.experimental import pallas as pl
+from jax.experimental.pallas import tpu as pltpu
 from jax.sharding import PartitionSpec as P
 
 HD = 128
@@ -151,9 +155,505 @@
     return result.transpose(1, 0, 2).reshape(tok_rows, heads_dev * head_size).astype(jnp.bfloat16)
 
 
+def fused_kernel(
+    n_s,
+    n_m,
+    groups,
+    seg_ref,
+    lat_ref,
+    conv_ref,
+    embed_ref,
+    text_ref,
+    w_ref,
+    out_ref,
+    w_buf,
+    halo,
+    ew,
+    text_buf,
+    patch_buf,
+    emb_pad,
+    emb_out,
+    hid_buf,
+    acc,
+    qkv_out,
+    qkv_buf,
+    attn_out,
+    attn_buf,
+    w_sem,
+    halo_send,
+    halo_recv,
+    ew_send,
+    ew_recv,
+    text_send,
+    text_recv,
+    patch_send,
+    patch_recv,
+    hid_send,
+    hid_recv,
+    qkv_send,
+    qkv_recv,
+    attn_send,
+    attn_recv,
+):
+    ranks = n_s // groups
+    s = lax.axis_index("seq")
+    m = lax.axis_index("mp")
+    g = s // ranks
+    r = s % ranks
+    far = (m + 2) % n_m
+    near = m + 1 - 2 * (m % 2)
+    cols = lat_ref.shape[1]
+    chans = lat_ref.shape[2]
+    chan_dev = conv_ref.shape[2]
+    half = cols // 2
+    tok_rows = text_ref.shape[0]
+    width = ew.shape[2]
+    img_toks = n_s * half
+    total_len = n_s * tok_rows
+    pending = []
+
+    def push(src, dst, send, recv, seq, mp):
+        copy = pltpu.make_async_remote_copy(
+            src_ref=src,
+            dst_ref=dst,
+            send_sem=send,
+            recv_sem=recv,
+            device_id=(seq, mp),
+            device_id_type=pl.DeviceIdType.MESH,
+        )
+        copy.start()
+        pending.append(copy)
+
+    def arrived(dst, send, recv):
+        pltpu.make_async_remote_copy(
+            src_ref=dst,
+            dst_ref=dst,
+            send_sem=send,
+            recv_sem=recv,
+            device_id=(s, near),
+            device_id_type=pl.DeviceIdType.MESH,
+        ).wait_recv()
+
+    w_copies = [
+        pltpu.make_async_copy(w_ref.at[part], w_buf.at[part], w_sem.at[part]) for part in range(3)
+    ]
+    for copy in w_copies:
+        copy.start()
+
+    barrier = pltpu.get_barrier_semaphore()
+    for step in range(1, n_s):
+        pl.semaphore_signal(
+            barrier, 1, device_id=((s + step) % n_s, m), device_id_type=pl.DeviceIdType.MESH
+        )
+    for step in range(1, n_m):
+        pl.semaphore_signal(
+            barrier, 1, device_id=(s, (m + step) % n_m), device_id_type=pl.DeviceIdType.MESH
+        )
+    pl.semaphore_wait(barrier, n_s + n_m - 2)
+
+    def edge(first, seq):
+        return pltpu.make_async_remote_copy(
+            src_ref=lat_ref.at[1 - first],
+            dst_ref=halo.at[first],
+            send_sem=halo_send.at[first],
+            recv_sem=halo_recv.at[first],
+            device_id=(seq, m),
+            device_id_type=pl.DeviceIdType.MESH,
+        )
+
+    @pl.when(s < n_s - 1)
+    def _():
+        edge(0, s + 1).start()
+
+    @pl.when(s > 0)
+    def _():
+        edge(1, s - 1).start()
+
+    for step in range(1, n_m):
+        peer = (m + step) % n_m
+        push(
+            embed_ref.at[:, pl.ds(pl.multiple_of(peer * width, width), width)],
+            ew.at[m],
+            ew_send.at[step - 1],
+            ew_recv.at[m],
+            s,
+            peer,
+        )
+    ew[m] = embed_ref[:, pl.ds(pl.multiple_of(m * width, width), width)]
+    push(text_ref, text_buf.at[m], text_send.at[0], text_recv.at[m], s, far)
+    push(text_ref, text_buf.at[m], text_send.at[1], text_recv.at[m], s, near)
+    text_buf[m] = text_ref[...]
+
+    start_unit = jnp.int32(0)
+    before = jnp.int32(1)
+    for unit in range((total_len - img_toks) // half):
+        before = before * (1 - seg_ref[unit * half])
+        start_unit = start_unit + before
+    start = start_unit * half
+
+    zero_row = jnp.zeros((cols, chans), jnp.bfloat16)
+
+    @pl.when(s == 0)
+    def _():
+        halo[0] = zero_row
+
+    @pl.when(s == n_s - 1)
+    def _():
+        halo[1] = zero_row
+
+    def one_hot(rows, columns, shift):
+        row = lax.broadcasted_iota(jnp.int32, (rows, columns), 0)
+        column = lax.broadcasted_iota(jnp.int32, (rows, columns), 1)
+        return jnp.where(column == shift(row), 1.0, 0.0).astype(jnp.bfloat16)
+
+    picks = one_hot(4 * half, cols, lambda row: 2 * (row % half) + row // half - 1)
+
+    def picked(row):
+        return jnp.dot(picks, row, preferred_element_type=jnp.float32).astype(jnp.bfloat16)
+
+    inner_rows = [picked(lat_ref[0]), picked(lat_ref[1])]
+
+    @pl.when(s > 0)
+    def _():
+        edge(0, s).wait_recv()
+
+    @pl.when(s < n_s - 1)
+    def _():
+        edge(1, s).wait_recv()
+
+    rows = [picked(halo[0]), *inner_rows, picked(halo[1])]
+    summed = jnp.zeros((4 * half, chan_dev), jnp.float32)
+    for row_step in range(3):
+        for col_step in range(3):
+            at = slice(col_step * half, (col_step + 2) * half)
+            window = jnp.concatenate([rows[row_step][at], rows[row_step + 1][at]], axis=0)
+            summed = summed + lax.dot_general(
+                window,
+                conv_ref[row_step, col_step],
+                (((1,), (1,)), ((), ())),
+                preferred_element_type=jnp.float32,
+            )
+    at = slice(half, 3 * half)
+    centre = jnp.concatenate([rows[1][at], rows[2][at]], axis=0)
+    row = lax.broadcasted_iota(jnp.int32, (chans, chan_dev), 0)
+    column = lax.broadcasted_iota(jnp.int32, (chans, chan_dev), 1)
+    own = jnp.where(row == column + m * chan_dev, 1.0, 0.0).astype(jnp.bfloat16)
+    own_chan = jnp.dot(centre, own, preferred_element_type=jnp.float32)
+    mixed = (own_chan + summed / (1.0 + jnp.exp(-summed))).astype(jnp.bfloat16)
+    patches = jnp.zeros((half, 4 * chan_dev), jnp.float32)
+    for cell in range(4):
+        place = one_hot(chan_dev, 4 * chan_dev, lambda row: row + cell * chan_dev)
+        patches = patches + jnp.dot(
+            mixed[cell * half : (cell + 1) * half], place, preferred_element_type=jnp.float32
+        )
+    patch_buf[s, m] = patches.astype(jnp.bfloat16)
+
+    sent = [0]
+
+    def send_patch(slot_s, slot_m, seq, mp):
+        push(
+            patch_buf.at[slot_s, slot_m],
+            patch_buf.at[slot_s, slot_m],
+            patch_send.at[sent[0]],
+            patch_recv.at[slot_s, slot_m],
+            seq,
+            mp,
+        )
+        sent[0] += 1
+
+    def wait_patch(slot_s, slot_m):
+        arrived(patch_buf.at[slot_s, slot_m], patch_send.at[0], patch_recv.at[slot_s, slot_m])
+
+    for step in range(1, groups):
+        send_patch(s, m, (g + step) % groups * ranks + r, m)
+    for group_step in range(groups):
+        slot = (g + group_step) % groups * ranks + r
+        if group_step:
+            wait_patch(slot, m)
+        for step in range(1, ranks):
+            send_patch(slot, m, g * ranks + (r + step) % ranks, m)
+        send_patch(slot, m, s, far)
+        send_patch(slot, m, s, near)
+    for group_step in range(groups):
+        for step in range(1, ranks):
+            slot = (g + group_step) % groups * ranks + (r + step) % ranks
+            wait_patch(slot, m)
+            send_patch(slot, m, s, far)
+            send_patch(slot, m, s, near)
+    for step in range(n_s):
+        slot = (s + step) % n_s
+        wait_patch(slot, far)
+        send_patch(slot, far, s, near)
+
+    arrived(text_buf.at[far], text_send.at[0], text_recv.at[far])
+    push(text_buf.at[far], text_buf.at[far], text_send.at[2], text_recv.at[far], s, near)
+    near_far = (near + 2) % n_m
+
+    for step in range(1, n_m):
+        peer = (m + step) % n_m
+        arrived(ew.at[peer], ew_send.at[0], ew_recv.at[peer])
+    for step in range(n_s):
+        slot = (s + step) % n_s
+        wait_patch(slot, near)
+        wait_patch(slot, near_far)
+    embedded = jnp.zeros((img_toks, width), jnp.float32)
+    for group in range(n_m):
+        embedded = embedded + jnp.dot(
+            patch_buf[:, group].reshape(img_toks, 4 * chan_dev),
+            ew[group],
+            preferred_element_type=jnp.float32,
+        )
+    pad = total_len - img_toks
+    pad_units = pad // half
+    blank = jnp.zeros((pad_units, half, width), jnp.bfloat16)
+    emb_pad[0:pad_units] = blank
+    emb_pad[pad_units : pad_units + n_s] = embedded.astype(jnp.bfloat16).reshape(n_s, half, width)
+    emb_pad[pad_units + n_s :] = blank
+
+    sent_hid = [0]
+
+    def send_hid(src, slot_s, slot_m, seq, mp):
+        push(
+            src,
+            hid_buf.at[slot_s, slot_m],
+            hid_send.at[sent_hid[0]],
+            hid_recv.at[slot_s, slot_m],
+            seq,
+            mp,
+        )
+        sent_hid[0] += 1
+
+    def wait_hid(slot_s, slot_m):
+        arrived(hid_buf.at[slot_s, slot_m], hid_send.at[0], hid_recv.at[slot_s, slot_m])
+
+    per_block = tok_rows // half
+
+    def put_block(ref, seq):
+        for unit in range(per_block):
+            ref[unit * half : (unit + 1) * half] = emb_pad[
+                pad_units + seq * per_block + unit - start_unit
+            ]
+
+    for step in range(1, n_s):
+        seq = (s + step) % n_s
+        put_block(emb_out.at[seq], seq)
+        send_hid(emb_out.at[seq], s, m, seq, m)
+    put_block(hid_buf.at[s, m], s)
+    for step in range(n_s):
+        slot = (s + n_s - step) % n_s
+        if step:
+            wait_hid(slot, m)
+        send_hid(hid_buf.at[slot, m], slot, m, s, far)
+        send_hid(hid_buf.at[slot, m], slot, m, s, near)
+    arrived(text_buf.at[near], text_send.at[0], text_recv.at[near])
+    arrived(text_buf.at[near_far], text_send.at[0], text_recv.at[near_far])
+    for copy in w_copies:
+        copy.wait()
+    my_pos = s * tok_rows + lax.broadcasted_iota(jnp.int32, (tok_rows, 1), 0)
+    is_image = (my_pos >= start) & (my_pos < start + img_toks)
+    head_cols = w_ref.shape[2]
+    per_text = text_ref.shape[1] // width
+    for step in range(n_s):
+        slot = (s + n_s - step) % n_s
+        wait_hid(slot, far)
+        send_hid(hid_buf.at[slot, far], slot, far, s, near)
+    for step in range(n_s):
+        slot = (s + n_s - step) % n_s
+        wait_hid(slot, near)
+        wait_hid(slot, near_far)
+        pieces = []
+        for group in range(n_m):
+            chunk = slot * n_m + group
+            text = text_buf[
+                chunk // per_text,
+                :,
+                pl.ds(pl.multiple_of(chunk % per_text * width, width), width),
+            ]
+            pieces.append(jnp.where(is_image, hid_buf[slot, group], text))
+        hidden = jnp.concatenate(pieces, axis=1)
+        deep = n_m * width
+        for part in range(3):
+            product = jnp.dot(
+                hidden,
+                w_buf[part, pl.ds(pl.multiple_of(slot * deep, deep), deep)],
+                preferred_element_type=jnp.float32,
+            )
+            if step == 0:
+                acc[part] = product
+            else:
+                acc[part] += product
+
+    for head in range(groups):
+        for part in range(3):
+            qkv_out[head, :, part * HD : (part + 1) * HD] = acc[
+                part, :, head * HD : (head + 1) * HD
+            ].astype(jnp.bfloat16)
+    sent_qkv = [0]
+
+    def send_qkv(src, dst, slot, seq):
+        push(src, dst, qkv_send.at[sent_qkv[0]], qkv_recv.at[slot], seq, m)
+        sent_qkv[0] += 1
+
+    for step in range(1, groups):
+        head = (g + step) % groups
+        send_qkv(qkv_out.at[head], qkv_buf.at[s], s, head * ranks + r)
+    qkv_buf[s] = qkv_out[g]
+    for group_step in range(groups):
+        slot = (g + groups - group_step) % groups * ranks + r
+        if group_step:
+            arrived(qkv_buf.at[slot], qkv_send.at[0], qkv_recv.at[slot])
+        kv = qkv_buf.at[slot, :, pl.ds(HD, 2 * HD)]
+        for step in range(1, ranks):
+            send_qkv(kv, kv, slot, g * ranks + (r + step) % ranks)
+    for group_step in range(groups):
+        for step in range(1, ranks):
+            slot = (g + groups - group_step) % groups * ranks + (r + step) % ranks
+            arrived(qkv_buf.at[slot, :, pl.ds(HD, 2 * HD)], qkv_send.at[0], qkv_recv.at[slot])
+
+    keys = qkv_buf[:, :, HD : 2 * HD].reshape(total_len, HD)
+    values = qkv_buf[:, :, 2 * HD :].reshape(total_len, HD)
+    key_pos = lax.broadcasted_iota(jnp.int32, (1, total_len), 1)
+    key_image = (key_pos >= start) & (key_pos < start + img_toks)
+    for group_step in [*range(1, groups), 0]:
+        other = (g + group_step) % groups
+        slot = other * ranks + r
+        query_pos = slot * tok_rows + lax.broadcasted_iota(jnp.int32, (tok_rows, 1), 0)
+        query_image = (query_pos >= start) & (query_pos < start + img_toks)
+        allowed = (key_pos <= query_pos) | (query_image & key_image)
+        scores = (
+            lax.dot_general(
+                qkv_buf[slot, :, :HD],
+                keys,
+                (((1,), (1,)), ((), ())),
+                preferred_element_type=jnp.float32,
+            )
+            * HD**-0.5
+        )
+        scores = jnp.where(allowed, scores, -1e30)
+        highest = jnp.max(scores, axis=1, keepdims=True)
+        weights = jnp.where(allowed, jnp.exp(scores - highest), 0.0)
+        totals = jnp.sum(weights, axis=1, keepdims=True)
+        result = jnp.dot(
+            weights.astype(jnp.bfloat16), values, preferred_element_type=jnp.float32
+        )
+        result = (result / totals).astype(jnp.bfloat16)
+        if group_step:
+            attn_out[other] = result
+            push(
+                attn_out.at[other],
+                attn_buf.at[g],
+                attn_send.at[group_step - 1],
+                attn_recv.at[g],
+                slot,
+                m,
+            )
+        else:
+            attn_buf[g] = result
+    for group_step in range(1, groups):
+        other = (g + group_step) % groups
+        arrived(attn_buf.at[other], attn_send.at[0], attn_recv.at[other])
+    for head in range(groups):
+        out_ref[:, head * HD : (head + 1) * HD] = attn_buf[head]
+
+    @pl.when(s < n_s - 1)
+    def _():
+        edge(0, s).wait_send()
+
+    @pl.when(s > 0)
+    def _():
+        edge(1, s).wait_send()
+
+    for copy in pending:
+        copy.wait_send()
+
+
+def fused_shards(latents, conv_w, embed_w, text_emb, wqkv, seg_ids):
+    n_s = lax.axis_size("seq")
+    n_m = lax.axis_size("mp")
+    tile_rows, cols, chans = latents.shape
+    chan_dev = conv_w.shape[3]
+    tok_rows, feats = text_emb.shape
+    groups = wqkv.shape[2] // HD
+    ranks = n_s // groups
+    width = embed_w.shape[2] // n_m
+    half = cols // 2
+    total_len = seg_ids.shape[0]
+    img_toks = n_s * half
+    bf16 = jnp.bfloat16
+    vmem = pl.BlockSpec(memory_space=pltpu.VMEM)
+    dma = pltpu.SemaphoreType.DMA
+    return pl.pallas_call(
+        functools.partial(fused_kernel, n_s, n_m, groups),
+        out_shape=jax.ShapeDtypeStruct((tok_rows, groups * HD), bf16),
+        in_specs=[
+            pl.BlockSpec(memory_space=pltpu.SMEM),
+            vmem,
+            vmem,
+            vmem,
+            vmem,
+            pl.BlockSpec(memory_space=pl.ANY),
+        ],
+        out_specs=vmem,
+        scratch_shapes=[
+            pltpu.VMEM((3, wqkv.shape[0], wqkv.shape[2]), bf16),
+            pltpu.VMEM((2, cols, chans), bf16),
+            pltpu.VMEM((n_m, 4 * chan_dev, width), bf16),
+            pltpu.VMEM((n_m, tok_rows, feats), bf16),
+            pltpu.VMEM((n_s, n_m, half, 4 * chan_dev), bf16),
+            pltpu.VMEM(((2 * total_len - img_toks) // half, half, width), bf16),
+            pltpu.VMEM((n_s, tok_rows, width), bf16),
+            pltpu.VMEM((n_s, n_m, tok_rows, width), bf16),
+            pltpu.VMEM((3, tok_rows, wqkv.shape[2]), jnp.float32),
+            pltpu.VMEM((groups, tok_rows, 3 * HD), bf16),
+            pltpu.VMEM((n_s, tok_rows, 3 * HD), bf16),
+            pltpu.VMEM((groups, tok_rows, HD), bf16),
+            pltpu.VMEM((groups, tok_rows, HD), bf16),
+            dma((3,)),
+            dma((2,)),
+            dma((2,)),
+            dma((n_m - 1,)),
+            dma((n_m,)),
+            dma((3,)),
+            dma((n_m,)),
+            dma((groups - 1 + groups * (ranks - 1) + 3 * n_s,)),
+            dma((n_s, n_m)),
+            dma((n_s - 1 + 3 * n_s,)),
+            dma((n_s, n_m)),
+            dma((groups - 1 + groups * (ranks - 1),)),
+            dma((n_s,)),
+            dma((groups - 1,)),
+            dma((groups,)),
+        ],
+        compiler_params=pltpu.CompilerParams(
+            collective_id=0, has_side_effects=True, vmem_limit_bytes=48 * 1024 * 1024
+        ),
+        cost_estimate=pl.CostEstimate(
+            flops=2 * tok_rows * wqkv.shape[0] * 3 * wqkv.shape[2],
+            bytes_accessed=2 * wqkv.shape[0] * 3 * wqkv.shape[2],
+            transcendentals=tok_rows * total_len * groups,
+        ),
+    )(
+        seg_ids,
+        latents,
+        conv_w.transpose(0, 1, 3, 2),
+        embed_w.reshape(4 * chan_dev, embed_w.shape[2]),
+        text_emb,
+        wqkv.transpose(1, 0, 2),
+    )
+
+
+def run_shards(latents, conv_w, embed_w, text_emb, wqkv, seg_ids):
+    n_s = lax.axis_size("seq")
+    n_m = lax.axis_size("mp")
+    groups = wqkv.shape[2] // HD
+    fits = n_m == 4 and n_s % groups == 0 and embed_w.shape[2] % (n_m * HD) == 0
+    body = fused_shards if fits and latents.shape[0] == 2 else shards
+    return body(latents, conv_w, embed_w, text_emb, wqkv, seg_ids)
+
+
 def solution(mesh):
     return jax.shard_map(
-        shards,
+        run_shards,
         mesh=mesh,
         in_specs=(
             P("seq", None, None),

time: 213 us -> 63.2 us (0.30)
  waiting for transfers between devices: 77.1 us -> 0 us
  blocking collectives: 74.8 us -> 0 us
  Pallas kernels: 0 us -> 57.8 us
  matrix products: 16.7 us -> 0 us
  local copies, waits for them, and re-layouts: 21.1 us -> 5.11 us
  between operations: 13.3 us -> 0.01 us
  starting transfers between devices: 6.25 us -> 0 us
  other arithmetic: 2.6 us -> 0 us
    all_gather x3 -> x0, waiting for transfers between devices: 76.3 us -> none  [the longest x1 38.3 us: shards(): lax.all_gather(key_rows, 'seq', axis=0, tiled=True)]
    pallas_call x0 -> x1, Pallas kernels: none -> 57.8 us  [fused_shards(): pl.pallas_call(functools.partial(fused_kernel, n_s, n_m, groups), out_sha...]
    psum x1 -> x0, blocking collectives: 40.6 us -> none  [shards(): hidden = lax.psum(partial_emb, 'mp').astype(jnp.bfloat16)]
    all_gather x1 -> x0, blocking collectives: 34.2 us -> none  [shards(): piece = lax.all_gather(patches, 'seq', axis=0, tiled=True)]
    dot_general x13 -> x0, matrix products: 16.7 us -> none  [the longest x1 8.83 us: shards(): jnp.dot(hidden, wqkv.reshape(width, 3 * head_cols), preferred_element_typ...]
    unnamed x10 -> x11, local copies, waits for them, and re-layouts: 17.1 us -> 5.11 us
    ppermute x2 -> x0, starting transfers between devices: 6.17 us -> none  [the longest x1 4.87 us: padded_2(): lax.ppermute(tail, axis, [(i, (i + 1) % count) for i in range(ends)])]
  transfers between devices with their start and end apart: 5 -> 0, of which waited for: 3 -> 0; matrix products, arithmetic and copies ran while one was open for 12% -> 0% of each run, Pallas kernels for 0% -> 0%
where the time goes in v1:
time: 63.2 us; the launch traced here: 62.9 us
  Pallas kernels  57.8 us (91%)
  local copies, waits for them, and re-layouts  5.11 us (8%)
    pallas_call x1, Pallas kernels, fused_shards(): pl.pallas_call(functools.partial(fused_kernel, n_s, n_m, groups), out_sha...  57.8 us
    unnamed x11, local copies, waits for them, and re-layouts  5.11 us

profile of v1, /device:TPU:0, one launch (start us, length us, event | category | flops | bytes accessed | tf_op | source)
XLA Modules:
  0.0 62.9 jit_solution(1801423336664367533)
XLA Ops:
  0.0 0.0 copy-start
  0.0 1.0 %copy-done = bf16[3,3,256,64]{2,3,1,0:T(8,128)(2,1)S(1)} copy-done((bf16[3,3,256,64]{2,3,1,0:T(8,128)(2,1)S(1)}, bf16[3,3,256,64]{2,3,1,0:T(8,128)(2,1)}, u32[]{:S(2)}) %copy-start) | copy-done | bytes 294936
  1.0 0.0 copy-start.1
  1.0 0.9 %copy-done.1 = bf16[4,64,512]{2,1,0:T(8,128)(2,1)S(1)} copy-done((bf16[4,64,512]{2,1,0:T(8,128)(2,1)S(1)}, bf16[4,64,512]{2,1,0:T(8,128)(2,1)}, u32[]{:S(2)}) %copy-start.1) | copy-done | bytes 262168
  1.9 0.0 copy-start.2
  1.9 0.9 %copy-done.2 = bf16[128,1024]{1,0:T(8,128)(2,1)S(1)} copy-done((bf16[128,1024]{1,0:T(8,128)(2,1)S(1)}, bf16[128,1024]{1,0:T(8,128)(2,1)}, u32[]{:S(2)}) %copy-start.2) | copy-done | bytes 262168
  2.9 0.0 copy-start.3
  2.9 0.9 %copy-done.3 = bf16[2,128,256]{2,1,0:T(8,128)(2,1)S(1)} copy-done((bf16[2,128,256]{2,1,0:T(8,128)(2,1)S(1)}, bf16[2,128,256]{2,1,0:T(8,128)(2,1)}, u32[]{:S(2)}) %copy-start.3) | copy-done | bytes 131096
  3.8 0.0 copy-start.4
  3.8 0.7 %copy-done.4 = s32[1024]{0:T(1024)S(1)} copy-done((s32[1024]{0:T(1024)S(1)}, s32[1024]{0:T(1024)}, u32[]{:S(2)}) %copy-start.4) | copy-done | bytes 4120
  4.5 57.8 %shard_map.64 = bf16[128,512]{1,0:T(8,128)(2,1)S(1)} custom-call(s32[1024]{0:T(1024)S(1)} %copy-done.4, bf16[2,128,256]{2,1,0:T(8,128)(2,1)S(1)} %copy-done.3, bf16[3,3,64,256]{3,2,1,0:T(8,128)(2,1)S(1)} %bitcast.3, bf16[256,512]{1,0:T(8,128)(2,1)S(1)} %bitcast.4, bf16[128,1024]{1,0:T(8,128)(2,1)S(1)} %copy-done.2, bf16[3,4096,512]{2,1,0:T(8,128)(2,1)} %bitcast.5), custom_call_target="tpu_custom_call" | custom-call | flops 1610612736 | bytes 12582912 | tf_op jit(solution)/shard_map/pallas_call | solution.py:585
  62.3 0.7 %copy.8 = bf16[128,512]{1,0:T(8,128)(2,1)} copy(bf16[128,512]{1,0:T(8,128)(2,1)S(1)} %shard_map.64) | data formatting | bytes 262144
Async XLA Ops:
  0.0 1.0 %copy-start = (bf16[3,3,256,64]{2,3,1,0:T(8,128)(2,1)S(1)}, bf16[3,3,256,64]{2,3,1,0:T(8,128)(2,1)}, u32[]{:S(2)}) copy-start(bf16[3,3,256,64]{2,3,1,0:T(8,128)(2,1)} %param.7) | copy-start | bytes 884740
  1.0 0.9 %copy-start.1 = (bf16[4,64,512]{2,1,0:T(8,128)(2,1)S(1)}, bf16[4,64,512]{2,1,0:T(8,128)(2,1)}, u32[]{:S(2)}) copy-start(bf16[4,64,512]{2,1,0:T(8,128)(2,1)} %param.8) | copy-start | bytes 786436
  1.9 0.9 %copy-start.2 = (bf16[128,1024]{1,0:T(8,128)(2,1)S(1)}, bf16[128,1024]{1,0:T(8,128)(2,1)}, u32[]{:S(2)}) copy-start(bf16[128,1024]{1,0:T(8,128)(2,1)} %text_ref.1) | copy-start | bytes 786436
  2.9 0.9 %copy-start.3 = (bf16[2,128,256]{2,1,0:T(8,128)(2,1)S(1)}, bf16[2,128,256]{2,1,0:T(8,128)(2,1)}, u32[]{:S(2)}) copy-start(bf16[2,128,256]{2,1,0:T(8,128)(2,1)} %lat_ref.1) | copy-start | bytes 393220
  3.8 0.7 %copy-start.4 = (s32[1024]{0:T(1024)S(1)}, s32[1024]{0:T(1024)}, u32[]{:S(2)}) copy-start(s32[1024]{0:T(1024)} %seg_ref.1) | copy-start | bytes 12292

commit v2 on v1

--- a/solution.py
+++ b/solution.py
@@ -167,9 +167,12 @@
     w_ref,
     out_ref,
     w_buf,
+    lat_buf,
+    conv_buf,
     halo,
     ew,
     text_buf,
+    patch_out,
     patch_buf,
     emb_pad,
     emb_out,
@@ -179,6 +182,7 @@
     qkv_buf,
     attn_out,
     attn_buf,
+    load_sem,
     w_sem,
     halo_send,
     halo_recv,
@@ -187,9 +191,11 @@
     text_send,
     text_recv,
     patch_send,
+    far_recv,
     patch_recv,
     hid_send,
     hid_recv,
+    near_recv,
     qkv_send,
     qkv_recv,
     attn_send,
@@ -201,7 +207,10 @@
     g = s // ranks
     r = s % ranks
     far = (m + 2) % n_m
-    near = m + 1 - 2 * (m % 2)
+    x = m // 2
+    c = m % 2
+    near = m + 1 - 2 * c
+    near_far = (near + 2) % n_m
     cols = lat_ref.shape[1]
     chans = lat_ref.shape[2]
     chan_dev = conv_ref.shape[2]
@@ -212,6 +221,9 @@
     total_len = n_s * tok_rows
     pending = []
 
+    def my_cols(core):
+        return pl.ds(pl.multiple_of(core * width, width), width)
+
     def push(src, dst, send, recv, seq, mp):
         copy = pltpu.make_async_remote_copy(
             src_ref=src,
@@ -234,6 +246,14 @@
             device_id_type=pl.DeviceIdType.MESH,
         ).wait_recv()
 
+    loads = [
+        pltpu.make_async_copy(lat_ref, lat_buf, load_sem.at[0]),
+        pltpu.make_async_copy(conv_ref, conv_buf, load_sem.at[1]),
+        pltpu.make_async_copy(embed_ref.at[:, my_cols(c)], ew.at[m], load_sem.at[2]),
+        pltpu.make_async_copy(text_ref, text_buf.at[m], load_sem.at[3]),
+    ]
+    for copy in loads:
+        copy.start()
     w_copies = [
         pltpu.make_async_copy(w_ref.at[part], w_buf.at[part], w_sem.at[part]) for part in range(3)
     ]
@@ -269,20 +289,15 @@
     def _():
         edge(1, s - 1).start()
 
-    for step in range(1, n_m):
-        peer = (m + step) % n_m
+    for at, peer in enumerate((far, near_far, near)):
         push(
-            embed_ref.at[:, pl.ds(pl.multiple_of(peer * width, width), width)],
+            embed_ref.at[:, my_cols(peer % 2)],
             ew.at[m],
-            ew_send.at[step - 1],
+            ew_send.at[at],
             ew_recv.at[m],
             s,
             peer,
         )
-    ew[m] = embed_ref[:, pl.ds(pl.multiple_of(m * width, width), width)]
-    push(text_ref, text_buf.at[m], text_send.at[0], text_recv.at[m], s, far)
-    push(text_ref, text_buf.at[m], text_send.at[1], text_recv.at[m], s, near)
-    text_buf[m] = text_ref[...]
 
     start_unit = jnp.int32(0)
     before = jnp.int32(1)
@@ -311,7 +326,33 @@
     def picked(row):
         return jnp.dot(picks, row, preferred_element_type=jnp.float32).astype(jnp.bfloat16)
 
-    inner_rows = [picked(lat_ref[0]), picked(lat_ref[1])]
+    def taps(row, row_step):
+        total = None
+        for col_step in range(3):
+            term = lax.dot_general(
+                row[col_step * half : (col_step + 2) * half],
+                conv_buf[row_step, col_step],
+                (((1,), (1,)), ((), ())),
+                preferred_element_type=jnp.float32,
+            )
+            total = term if total is None else total + term
+        return total
+
+    loads[0].wait()
+    loads[1].wait()
+    upper, lower = picked(lat_buf[0]), picked(lat_buf[1])
+    sums = [taps(upper, 1) + taps(lower, 2), taps(upper, 0) + taps(lower, 1)]
+    row = lax.broadcasted_iota(jnp.int32, (chans, chan_dev), 0)
+    column = lax.broadcasted_iota(jnp.int32, (chans, chan_dev), 1)
+    own = jnp.where(row == column + m * chan_dev, 1.0, 0.0).astype(jnp.bfloat16)
+    own_chan = [
+        jnp.dot(line[half : 3 * half], own, preferred_element_type=jnp.float32)
+        for line in (upper, lower)
+    ]
+    places = [
+        one_hot(chan_dev, 4 * chan_dev, lambda row, cell=cell: row + cell * chan_dev)
+        for cell in range(4)
+    ]
 
     @pl.when(s > 0)
     def _():
@@ -321,157 +362,147 @@
     def _():
         edge(1, s).wait_recv()
 
-    rows = [picked(halo[0]), *inner_rows, picked(halo[1])]
-    summed = jnp.zeros((4 * half, chan_dev), jnp.float32)
-    for row_step in range(3):
-        for col_step in range(3):
-            at = slice(col_step * half, (col_step + 2) * half)
-            window = jnp.concatenate([rows[row_step][at], rows[row_step + 1][at]], axis=0)
-            summed = summed + lax.dot_general(
-                window,
-                conv_ref[row_step, col_step],
-                (((1,), (1,)), ((), ())),
+    sums = [sums[0] + taps(picked(halo[0]), 0), sums[1] + taps(picked(halo[1]), 2)]
+    patches = jnp.zeros((half, 4 * chan_dev), jnp.float32)
+    for line in range(2):
+        mixed = (own_chan[line] + sums[line] / (1.0 + jnp.exp(-sums[line]))).astype(jnp.bfloat16)
+        for side in range(2):
+            patches = patches + jnp.dot(
+                mixed[side * half : (side + 1) * half],
+                places[2 * line + side],
                 preferred_element_type=jnp.float32,
             )
-    at = slice(half, 3 * half)
-    centre = jnp.concatenate([rows[1][at], rows[2][at]], axis=0)
-    row = lax.broadcasted_iota(jnp.int32, (chans, chan_dev), 0)
-    column = lax.broadcasted_iota(jnp.int32, (chans, chan_dev), 1)
-    own = jnp.where(row == column + m * chan_dev, 1.0, 0.0).astype(jnp.bfloat16)
-    own_chan = jnp.dot(centre, own, preferred_element_type=jnp.float32)
-    mixed = (own_chan + summed / (1.0 + jnp.exp(-summed))).astype(jnp.bfloat16)
-    patches = jnp.zeros((half, 4 * chan_dev), jnp.float32)
-    for cell in range(4):
-        place = one_hot(chan_dev, 4 * chan_dev, lambda row: row + cell * chan_dev)
-        patches = patches + jnp.dot(
-            mixed[cell * half : (cell + 1) * half], place, preferred_element_type=jnp.float32
-        )
-    patch_buf[s, m] = patches.astype(jnp.bfloat16)
-
-    sent = [0]
-
-    def send_patch(slot_s, slot_m, seq, mp):
+
+    quarter = half // 2
+    first_half = patches[:quarter].astype(jnp.bfloat16)
+    second_half = patches[quarter:].astype(jnp.bfloat16)
+    patch_buf[s, c, x] = jnp.where(x == 0, first_half, second_half)
+    patch_out[...] = jnp.where(x == 0, second_half, first_half)
+    push(patch_out, patch_buf.at[s, c, x], patch_send.at[0], far_recv.at[0], s, far)
+    sent = [1]
+
+    def send_patch(slot, seq, mp):
         push(
-            patch_buf.at[slot_s, slot_m],
-            patch_buf.at[slot_s, slot_m],
+            patch_buf.at[slot, c],
+            patch_buf.at[slot, c],
             patch_send.at[sent[0]],
-            patch_recv.at[slot_s, slot_m],
+            patch_recv.at[slot, c],
             seq,
             mp,
         )
         sent[0] += 1
 
-    def wait_patch(slot_s, slot_m):
-        arrived(patch_buf.at[slot_s, slot_m], patch_send.at[0], patch_recv.at[slot_s, slot_m])
-
+    def wait_patch(slot, core):
+        arrived(patch_buf.at[slot, core], patch_send.at[0], patch_recv.at[slot, core])
+
+    arrived(patch_buf.at[s, c, 1 - x], patch_send.at[0], far_recv.at[0])
     for step in range(1, groups):
-        send_patch(s, m, (g + step) % groups * ranks + r, m)
+        send_patch(s, (g + step) % groups * ranks + r, m)
     for group_step in range(groups):
         slot = (g + group_step) % groups * ranks + r
         if group_step:
-            wait_patch(slot, m)
+            wait_patch(slot, c)
         for step in range(1, ranks):
-            send_patch(slot, m, g * ranks + (r + step) % ranks, m)
-        send_patch(slot, m, s, far)
-        send_patch(slot, m, s, near)
+            send_patch(slot, g * ranks + (r + step) % ranks, m)
+        send_patch(slot, s, near)
+        if group_step == 0:
+            push(text_ref, text_buf.at[m], text_send.at[0], text_recv.at[m], s, far)
+            push(text_ref, text_buf.at[m], text_send.at[1], text_recv.at[m], s, near)
     for group_step in range(groups):
         for step in range(1, ranks):
             slot = (g + group_step) % groups * ranks + (r + step) % ranks
-            wait_patch(slot, m)
-            send_patch(slot, m, s, far)
-            send_patch(slot, m, s, near)
-    for step in range(n_s):
-        slot = (s + step) % n_s
-        wait_patch(slot, far)
-        send_patch(slot, far, s, near)
-
-    arrived(text_buf.at[far], text_send.at[0], text_recv.at[far])
-    push(text_buf.at[far], text_buf.at[far], text_send.at[2], text_recv.at[far], s, near)
-    near_far = (near + 2) % n_m
-
-    for step in range(1, n_m):
-        peer = (m + step) % n_m
+            wait_patch(slot, c)
+            send_patch(slot, s, near)
+
+    loads[2].wait()
+    for peer in (far, near_far, near):
         arrived(ew.at[peer], ew_send.at[0], ew_recv.at[peer])
     for step in range(n_s):
-        slot = (s + step) % n_s
-        wait_patch(slot, near)
-        wait_patch(slot, near_far)
-    embedded = jnp.zeros((img_toks, width), jnp.float32)
+        wait_patch((s + step) % n_s, 1 - c)
+    embedded = jnp.zeros((n_s * quarter, width), jnp.float32)
     for group in range(n_m):
         embedded = embedded + jnp.dot(
-            patch_buf[:, group].reshape(img_toks, 4 * chan_dev),
+            patch_buf[:, group % 2, group // 2].reshape(n_s * quarter, 4 * chan_dev),
             ew[group],
             preferred_element_type=jnp.float32,
         )
-    pad = total_len - img_toks
-    pad_units = pad // half
-    blank = jnp.zeros((pad_units, half, width), jnp.bfloat16)
+    pad_units = (total_len - img_toks) // half
+    blank = jnp.zeros((pad_units, quarter, width), jnp.bfloat16)
     emb_pad[0:pad_units] = blank
-    emb_pad[pad_units : pad_units + n_s] = embedded.astype(jnp.bfloat16).reshape(n_s, half, width)
+    emb_pad[pad_units : pad_units + n_s] = embedded.astype(jnp.bfloat16).reshape(
+        n_s, quarter, width
+    )
     emb_pad[pad_units + n_s :] = blank
-
-    sent_hid = [0]
-
-    def send_hid(src, slot_s, slot_m, seq, mp):
-        push(
-            src,
-            hid_buf.at[slot_s, slot_m],
-            hid_send.at[sent_hid[0]],
-            hid_recv.at[slot_s, slot_m],
-            seq,
-            mp,
-        )
-        sent_hid[0] += 1
-
-    def wait_hid(slot_s, slot_m):
-        arrived(hid_buf.at[slot_s, slot_m], hid_send.at[0], hid_recv.at[slot_s, slot_m])
 
     per_block = tok_rows // half
 
     def put_block(ref, seq):
         for unit in range(per_block):
-            ref[unit * half : (unit + 1) * half] = emb_pad[
-                pad_units + seq * per_block + unit - start_unit
-            ]
+            ref[unit] = emb_pad[pad_units + seq * per_block + unit - start_unit]
 
     for step in range(1, n_s):
         seq = (s + step) % n_s
         put_block(emb_out.at[seq], seq)
-        send_hid(emb_out.at[seq], s, m, seq, m)
-    put_block(hid_buf.at[s, m], s)
+        push(
+            emb_out.at[seq],
+            hid_buf.at[s, c, x],
+            hid_send.at[step - 1],
+            hid_recv.at[s, x],
+            seq,
+            m,
+        )
+    put_block(hid_buf.at[s, c, x], s)
     for step in range(n_s):
         slot = (s + n_s - step) % n_s
         if step:
-            wait_hid(slot, m)
-        send_hid(hid_buf.at[slot, m], slot, m, s, far)
-        send_hid(hid_buf.at[slot, m], slot, m, s, near)
+            arrived(hid_buf.at[slot, c, x], hid_send.at[0], hid_recv.at[slot, x])
+        push(
+            hid_buf.at[slot, c, x],
+            hid_buf.at[slot, c, x],
+            hid_send.at[n_s - 1 + step],
+            hid_recv.at[slot, x],
+            s,
+            far,
+        )
+    loads[3].wait()
+    arrived(text_buf.at[far], text_send.at[0], text_recv.at[far])
+    push(text_buf.at[far], text_buf.at[far], text_send.at[2], text_recv.at[far], s, near)
+    for step in range(n_s):
+        slot = (s + n_s - step) % n_s
+        arrived(hid_buf.at[slot, c, 1 - x], hid_send.at[0], hid_recv.at[slot, 1 - x])
+        push(
+            hid_buf.at[slot, c],
+            hid_buf.at[slot, c],
+            hid_send.at[2 * n_s - 1 + step],
+            near_recv.at[slot],
+            s,
+            near,
+        )
     arrived(text_buf.at[near], text_send.at[0], text_recv.at[near])
     arrived(text_buf.at[near_far], text_send.at[0], text_recv.at[near_far])
     for copy in w_copies:
         copy.wait()
     my_pos = s * tok_rows + lax.broadcasted_iota(jnp.int32, (tok_rows, 1), 0)
     is_image = (my_pos >= start) & (my_pos < start + img_toks)
-    head_cols = w_ref.shape[2]
     per_text = text_ref.shape[1] // width
+    deep = 2 * width
     for step in range(n_s):
         slot = (s + n_s - step) % n_s
-        wait_hid(slot, far)
-        send_hid(hid_buf.at[slot, far], slot, far, s, near)
-    for step in range(n_s):
-        slot = (s + n_s - step) % n_s
-        wait_hid(slot, near)
-        wait_hid(slot, near_far)
+        arrived(hid_buf.at[slot, 1 - c], hid_send.at[0], near_recv.at[slot])
         pieces = []
-        for group in range(n_m):
-            chunk = slot * n_m + group
+        for core in range(2):
+            chunk = slot * 2 + core
             text = text_buf[
                 chunk // per_text,
                 :,
                 pl.ds(pl.multiple_of(chunk % per_text * width, width), width),
             ]
-            pieces.append(jnp.where(is_image, hid_buf[slot, group], text))
+            image = jnp.concatenate(
+                [hid_buf[slot, core, side, unit] for unit in range(per_block) for side in range(2)],
+                axis=0,
+            )
+            pieces.append(jnp.where(is_image, image, text))
         hidden = jnp.concatenate(pieces, axis=1)
-        deep = n_m * width
         for part in range(3):
             product = jnp.dot(
                 hidden,
@@ -575,39 +606,44 @@
     tok_rows, feats = text_emb.shape
     groups = wqkv.shape[2] // HD
     ranks = n_s // groups
-    width = embed_w.shape[2] // n_m
+    width = embed_w.shape[2] // 2
     half = cols // 2
     total_len = seg_ids.shape[0]
     img_toks = n_s * half
     bf16 = jnp.bfloat16
     vmem = pl.BlockSpec(memory_space=pltpu.VMEM)
+    hbm = pl.BlockSpec(memory_space=pltpu.HBM)
     dma = pltpu.SemaphoreType.DMA
     return pl.pallas_call(
         functools.partial(fused_kernel, n_s, n_m, groups),
         out_shape=jax.ShapeDtypeStruct((tok_rows, groups * HD), bf16),
         in_specs=[
             pl.BlockSpec(memory_space=pltpu.SMEM),
-            vmem,
-            vmem,
-            vmem,
-            vmem,
-            pl.BlockSpec(memory_space=pl.ANY),
+            hbm,
+            hbm,
+            hbm,
+            hbm,
+            hbm,
         ],
         out_specs=vmem,
         scratch_shapes=[
             pltpu.VMEM((3, wqkv.shape[0], wqkv.shape[2]), bf16),
             pltpu.VMEM((2, cols, chans), bf16),
+            pltpu.VMEM((3, 3, chan_dev, chans), bf16),
+            pltpu.VMEM((2, cols, chans), bf16),
             pltpu.VMEM((n_m, 4 * chan_dev, width), bf16),
             pltpu.VMEM((n_m, tok_rows, feats), bf16),
-            pltpu.VMEM((n_s, n_m, half, 4 * chan_dev), bf16),
-            pltpu.VMEM(((2 * total_len - img_toks) // half, half, width), bf16),
-            pltpu.VMEM((n_s, tok_rows, width), bf16),
-            pltpu.VMEM((n_s, n_m, tok_rows, width), bf16),
+            pltpu.VMEM((half // 2, 4 * chan_dev), bf16),
+            pltpu.VMEM((n_s, 2, 2, half // 2, 4 * chan_dev), bf16),
+            pltpu.VMEM(((2 * total_len - img_toks) // half, half // 2, width), bf16),
+            pltpu.VMEM((n_s, tok_rows // half, half // 2, width), bf16),
+            pltpu.VMEM((n_s, 2, 2, tok_rows // half, half // 2, width), bf16),
             pltpu.VMEM((3, tok_rows, wqkv.shape[2]), jnp.float32),
             pltpu.VMEM((groups, tok_rows, 3 * HD), bf16),
             pltpu.VMEM((n_s, tok_rows, 3 * HD), bf16),
             pltpu.VMEM((groups, tok_rows, HD), bf16),
             pltpu.VMEM((groups, tok_rows, HD), bf16),
+            dma((4,)),
             dma((3,)),
             dma((2,)),
             dma((2,)),
@@ -615,17 +651,19 @@
             dma((n_m,)),
             dma((3,)),
             dma((n_m,)),
-            dma((groups - 1 + groups * (ranks - 1) + 3 * n_s,)),
-            dma((n_s, n_m)),
-            dma((n_s - 1 + 3 * n_s,)),
-            dma((n_s, n_m)),
+            dma((1 + groups - 1 + groups * (ranks - 1) + n_s,)),
+            dma((1,)),
+            dma((n_s, 2)),
+            dma((n_s - 1 + 2 * n_s,)),
+            dma((n_s, 2)),
+            dma((n_s,)),
             dma((groups - 1 + groups * (ranks - 1),)),
             dma((n_s,)),
             dma((groups - 1,)),
             dma((groups,)),
         ],
         compiler_params=pltpu.CompilerParams(
-            collective_id=0, has_side_effects=True, vmem_limit_bytes=48 * 1024 * 1024
+            collective_id=0, has_side_effects=True, vmem_limit_bytes=60 * 1024 * 1024
         ),
         cost_estimate=pl.CostEstimate(
             flops=2 * tok_rows * wqkv.shape[0] * 3 * wqkv.shape[2],
@@ -646,7 +684,7 @@
     n_s = lax.axis_size("seq")
     n_m = lax.axis_size("mp")
     groups = wqkv.shape[2] // HD
-    fits = n_m == 4 and n_s % groups == 0 and embed_w.shape[2] % (n_m * HD) == 0
+    fits = n_m == 4 and n_s % groups == 0 and embed_w.shape[2] % (2 * HD) == 0
     body = fused_shards if fits and latents.shape[0] == 2 else shards
     return body(latents, conv_w, embed_w, text_emb, wqkv, seg_ids)
 

time: 63.2 us -> 60.3 us (0.954)
  local copies, waits for them, and re-layouts: 5.11 us -> 1.57 us
  Pallas kernels: 57.8 us -> 58.5 us
    unnamed x11 -> x1, local copies, waits for them, and re-layouts: 5.11 us -> 1.57 us
    pallas_call x1, Pallas kernels: 57.8 us -> 58.5 us  [fused_shards(): pl.pallas_call(functools.partial(fused_kernel, n_s, n_m, groups), out_sha...]
where the time goes in v2:
time: 60.3 us; the launch traced here: 60.1 us
  Pallas kernels  58.5 us (97%)
  local copies, waits for them, and re-layouts  1.57 us (3%)
    pallas_call x1, Pallas kernels, fused_shards(): pl.pallas_call(functools.partial(fused_kernel, n_s, n_m, groups), out_sha...  58.5 us
    unnamed x1, local copies, waits for them, and re-layouts  1.57 us

profile of v2, /device:TPU:0, one launch (start us, length us, event | category | flops | bytes accessed | tf_op | source)
XLA Modules:
  0.0 60.1 jit_solution(1409269705481343532)
XLA Ops:
  0.0 58.5 %shard_map.64 = bf16[128,512]{1,0:T(8,128)(2,1)} custom-call(s32[1024]{0:T(1024)} %seg_ref.1, bf16[2,128,256]{2,1,0:T(8,128)(2,1)} %lat_ref.1, bf16[3,3,64,256]{3,2,1,0:T(8,128)(2,1)} %bitcast.4, bf16[256,512]{1,0:T(8,128)(2,1)} %bitcast.5, bf16[128,1024]{1,0:T(8,128)(2,1)} %text_ref.1, bf16[3,4096,512]{2,1,0:T(8,128)(2,1)} %bitcast.3), custom_call_target="tpu_custom_call" | custom-call | flops 1610612736 | bytes 12582912 | tf_op jit(solution)/shard_map/pallas_call | solution.py:617
  58.5 1.6 %copy.8 = bf16[128,512]{1,0:T(8,128)(2,1)} copy(bf16[128,512]{1,0:T(8,128)(2,1)} %shard_map.64) | data formatting | bytes 262144

commit v3 on v2

--- a/solution.py
+++ b/solution.py
@@ -1,4 +1,5 @@
 import functools
+import math
 
 import jax
 import jax.numpy as jnp
@@ -180,6 +181,8 @@
     acc,
     qkv_out,
     qkv_buf,
+    score_buf,
+    prob_buf,
     attn_out,
     attn_buf,
     load_sem,
@@ -198,6 +201,8 @@
     near_recv,
     qkv_send,
     qkv_recv,
+    query_send,
+    query_recv,
     attn_send,
     attn_recv,
 ):
@@ -254,12 +259,6 @@
     ]
     for copy in loads:
         copy.start()
-    w_copies = [
-        pltpu.make_async_copy(w_ref.at[part], w_buf.at[part], w_sem.at[part]) for part in range(3)
-    ]
-    for copy in w_copies:
-        copy.start()
-
     barrier = pltpu.get_barrier_semaphore()
     for step in range(1, n_s):
         pl.semaphore_signal(
@@ -271,9 +270,11 @@
         )
     pl.semaphore_wait(barrier, n_s + n_m - 2)
 
+    loads[0].wait()
+
     def edge(first, seq):
         return pltpu.make_async_remote_copy(
-            src_ref=lat_ref.at[1 - first],
+            src_ref=lat_buf.at[1 - first],
             dst_ref=halo.at[first],
             send_sem=halo_send.at[first],
             recv_sem=halo_recv.at[first],
@@ -338,7 +339,6 @@
             total = term if total is None else total + term
         return total
 
-    loads[0].wait()
     loads[1].wait()
     upper, lower = picked(lat_buf[0]), picked(lat_buf[1])
     sums = [taps(upper, 1) + taps(lower, 2), taps(upper, 0) + taps(lower, 1)]
@@ -379,6 +379,12 @@
     patch_buf[s, c, x] = jnp.where(x == 0, first_half, second_half)
     patch_out[...] = jnp.where(x == 0, second_half, first_half)
     push(patch_out, patch_buf.at[s, c, x], patch_send.at[0], far_recv.at[0], s, far)
+    w_copies = [
+        pltpu.make_async_copy(w_ref.at[part], w_buf.at[part], w_sem.at[part]) for part in range(3)
+    ]
+    for copy in w_copies:
+        copy.start()
+
     sent = [1]
 
     def send_patch(slot, seq, mp):
@@ -525,49 +531,82 @@
         push(src, dst, qkv_send.at[sent_qkv[0]], qkv_recv.at[slot], seq, m)
         sent_qkv[0] += 1
 
+    key_cols = pl.ds(HD, 2 * HD)
+    query_cols = pl.ds(0, HD)
     for step in range(1, groups):
         head = (g + step) % groups
-        send_qkv(qkv_out.at[head], qkv_buf.at[s], s, head * ranks + r)
+        send_qkv(
+            qkv_out.at[head, :, key_cols], qkv_buf.at[s, :, key_cols], s, head * ranks + r
+        )
     qkv_buf[s] = qkv_out[g]
-    for group_step in range(groups):
+    for step in range(1, ranks):
+        kv = qkv_buf.at[s, :, key_cols]
+        send_qkv(kv, kv, s, g * ranks + (r + step) % ranks)
+    for step in range(1, groups):
+        head = (g + step) % groups
+        push(
+            qkv_out.at[head, :, query_cols],
+            qkv_buf.at[s, :, query_cols],
+            query_send.at[step - 1],
+            query_recv.at[s],
+            head * ranks + r,
+            m,
+        )
+    for group_step in range(1, groups):
         slot = (g + groups - group_step) % groups * ranks + r
-        if group_step:
-            arrived(qkv_buf.at[slot], qkv_send.at[0], qkv_recv.at[slot])
-        kv = qkv_buf.at[slot, :, pl.ds(HD, 2 * HD)]
+        kv = qkv_buf.at[slot, :, key_cols]
+        arrived(kv, qkv_send.at[0], qkv_recv.at[slot])
         for step in range(1, ranks):
             send_qkv(kv, kv, slot, g * ranks + (r + step) % ranks)
+
+    done = len(pending) - groups * ranks - groups
+    for copy in pending[:done]:
+        copy.wait_send()
+    del pending[:done]
+
+    @pl.when(s < n_s - 1)
+    def _():
+        edge(0, s).wait_send()
+
+    @pl.when(s > 0)
+    def _():
+        edge(1, s).wait_send()
+
+    for group_step in range(1, groups):
+        slot = (g + groups - group_step) % groups * ranks + r
+        arrived(qkv_buf.at[slot, :, query_cols], query_send.at[0], query_recv.at[slot])
     for group_step in range(groups):
         for step in range(1, ranks):
             slot = (g + groups - group_step) % groups * ranks + (r + step) % ranks
-            arrived(qkv_buf.at[slot, :, pl.ds(HD, 2 * HD)], qkv_send.at[0], qkv_recv.at[slot])
+            arrived(qkv_buf.at[slot, :, key_cols], qkv_send.at[0], qkv_recv.at[slot])
 
     keys = qkv_buf[:, :, HD : 2 * HD].reshape(total_len, HD)
     values = qkv_buf[:, :, 2 * HD :].reshape(total_len, HD)
-    key_pos = lax.broadcasted_iota(jnp.int32, (1, total_len), 1)
-    key_image = (key_pos >= start) & (key_pos < start + img_toks)
-    for group_step in [*range(1, groups), 0]:
+    order = [*range(1, groups), 0]
+    queries = jnp.concatenate(
+        [qkv_buf[(g + step) % groups * ranks + r, :, :HD] for step in order], axis=0
+    )
+    score_buf[...] = lax.dot_general(
+        queries, keys, (((1,), (1,)), ((), ())), preferred_element_type=jnp.float32
+    )
+    tile = min(32, tok_rows)
+    key_pos = lax.broadcasted_iota(jnp.int32, (tile, total_len), 1)
+    for at, group_step in enumerate(order):
         other = (g + group_step) % groups
         slot = other * ranks + r
-        query_pos = slot * tok_rows + lax.broadcasted_iota(jnp.int32, (tok_rows, 1), 0)
-        query_image = (query_pos >= start) & (query_pos < start + img_toks)
-        allowed = (key_pos <= query_pos) | (query_image & key_image)
-        scores = (
-            lax.dot_general(
-                qkv_buf[slot, :, :HD],
-                keys,
-                (((1,), (1,)), ((), ())),
-                preferred_element_type=jnp.float32,
-            )
-            * HD**-0.5
-        )
-        scores = jnp.where(allowed, scores, -1e30)
-        highest = jnp.max(scores, axis=1, keepdims=True)
-        weights = jnp.where(allowed, jnp.exp(scores - highest), 0.0)
-        totals = jnp.sum(weights, axis=1, keepdims=True)
-        result = jnp.dot(
-            weights.astype(jnp.bfloat16), values, preferred_element_type=jnp.float32
-        )
-        result = (result / totals).astype(jnp.bfloat16)
+        totals = []
+        for row in range(0, tok_rows, tile):
+            query_pos = slot * tok_rows + row + lax.broadcasted_iota(jnp.int32, (tile, 1), 0)
+            query_image = (query_pos >= start) & (query_pos < start + img_toks)
+            last_seen = jnp.where(query_image, start + img_toks - 1, query_pos)
+            scores = score_buf[at * tok_rows + row : at * tok_rows + row + tile]
+            scores = jnp.where(key_pos <= last_seen, scores, -1e30)
+            highest = jnp.max(scores, axis=1, keepdims=True)
+            weights = jnp.exp2((scores - highest) * (HD**-0.5 * math.log2(math.e)))
+            totals.append(jnp.sum(weights, axis=1, keepdims=True))
+            prob_buf[row : row + tile] = weights.astype(jnp.bfloat16)
+        result = jnp.dot(prob_buf[...], values, preferred_element_type=jnp.float32)
+        result = (result / jnp.concatenate(totals, axis=0)).astype(jnp.bfloat16)
         if group_step:
             attn_out[other] = result
             push(
@@ -585,15 +624,6 @@
         arrived(attn_buf.at[other], attn_send.at[0], attn_recv.at[other])
     for head in range(groups):
         out_ref[:, head * HD : (head + 1) * HD] = attn_buf[head]
-
-    @pl.when(s < n_s - 1)
-    def _():
-        edge(0, s).wait_send()
-
-    @pl.when(s > 0)
-    def _():
-        edge(1, s).wait_send()
-
     for copy in pending:
         copy.wait_send()
 
@@ -641,6 +671,8 @@
             pltpu.VMEM((3, tok_rows, wqkv.shape[2]), jnp.float32),
             pltpu.VMEM((groups, tok_rows, 3 * HD), bf16),
             pltpu.VMEM((n_s, tok_rows, 3 * HD), bf16),
+            pltpu.VMEM((groups * tok_rows, total_len), jnp.float32),
+            pltpu.VMEM((tok_rows, total_len), bf16),
             pltpu.VMEM((groups, tok_rows, HD), bf16),
             pltpu.VMEM((groups, tok_rows, HD), bf16),
             dma((4,)),
@@ -660,6 +692,8 @@
             dma((groups - 1 + groups * (ranks - 1),)),
             dma((n_s,)),
             dma((groups - 1,)),
+            dma((n_s,)),
+            dma((groups - 1,)),
             dma((groups,)),
         ],
         compiler_params=pltpu.CompilerParams(

time: 60.3 us -> 59.5 us (0.987)
  Pallas kernels: 58.5 us -> 57.7 us
    pallas_call x1, Pallas kernels: 58.5 us -> 57.7 us  [fused_shards(): pl.pallas_call(functools.partial(fused_kernel, n_s, n_m, groups), out_sha...]
where the time goes in v3:
time: 59.5 us; the launch traced here: 59.3 us
  Pallas kernels  57.7 us (97%)
  local copies, waits for them, and re-layouts  1.57 us (3%)
    pallas_call x1, Pallas kernels, fused_shards(): pl.pallas_call(functools.partial(fused_kernel, n_s, n_m, groups), out_sha...  57.7 us
    unnamed x1, local copies, waits for them, and re-layouts  1.57 us

profile of v3, /device:TPU:0, one launch (start us, length us, event | category | flops | bytes accessed | tf_op | source)
XLA Modules:
  0.0 59.3 jit_solution(10754806113811100264)
XLA Ops:
  0.0 57.7 %shard_map.64 = bf16[128,512]{1,0:T(8,128)(2,1)} custom-call(s32[1024]{0:T(1024)} %seg_ref.1, bf16[2,128,256]{2,1,0:T(8,128)(2,1)} %lat_ref.1, bf16[3,3,64,256]{3,2,1,0:T(8,128)(2,1)} %bitcast.4, bf16[256,512]{1,0:T(8,128)(2,1)} %bitcast.5, bf16[128,1024]{1,0:T(8,128)(2,1)} %text_ref.1, bf16[3,4096,512]{2,1,0:T(8,128)(2,1)} %bitcast.3), custom_call_target="tpu_custom_call" | custom-call | flops 1610612736 | bytes 12582912 | tf_op jit(solution)/shard_map/pallas_call | solution.py:647
  57.7 1.6 %copy.8 = bf16[128,512]{1,0:T(8,128)(2,1)} copy(bf16[128,512]{1,0:T(8,128)(2,1)} %shard_map.64) | data formatting | bytes 262144

commit v4 on v3

--- a/solution.py
+++ b/solution.py
@@ -194,7 +194,7 @@
     text_send,
     text_recv,
     patch_send,
-    far_recv,
+    half_recv,
     patch_recv,
     hid_send,
     hid_recv,
@@ -268,7 +268,10 @@
         pl.semaphore_signal(
             barrier, 1, device_id=(s, (m + step) % n_m), device_id_type=pl.DeviceIdType.MESH
         )
-    pl.semaphore_wait(barrier, n_s + n_m - 2)
+    for step in range(1, groups):
+        seq = (g + step) % groups * ranks + r
+        pl.semaphore_signal(barrier, 1, device_id=(seq, far), device_id_type=pl.DeviceIdType.MESH)
+    pl.semaphore_wait(barrier, n_s + n_m + groups - 3)
 
     loads[0].wait()
 
@@ -299,6 +302,8 @@
             s,
             peer,
         )
+
+    push(text_ref, text_buf.at[m], text_send.at[1], text_recv.at[m], s, near)
 
     start_unit = jnp.int32(0)
     before = jnp.int32(1)
@@ -378,47 +383,45 @@
     second_half = patches[quarter:].astype(jnp.bfloat16)
     patch_buf[s, c, x] = jnp.where(x == 0, first_half, second_half)
     patch_out[...] = jnp.where(x == 0, second_half, first_half)
-    push(patch_out, patch_buf.at[s, c, x], patch_send.at[0], far_recv.at[0], s, far)
+    sent = [0]
+
+    def send_patch(src, dst, recv, seq, mp):
+        push(src, dst, patch_send.at[sent[0]], recv, seq, mp)
+        sent[0] += 1
+
+    own_slot = patch_buf.at[s, c, x]
+    send_patch(patch_out, own_slot, half_recv.at[s, x], s, far)
+    for step in range(1, groups):
+        seq = (g + step) % groups * ranks + r
+        send_patch(own_slot, own_slot, half_recv.at[s, x], seq, m)
+        send_patch(patch_out, own_slot, half_recv.at[s, x], seq, far)
+    push(text_ref, text_buf.at[m], text_send.at[0], text_recv.at[m], s, far)
     w_copies = [
         pltpu.make_async_copy(w_ref.at[part], w_buf.at[part], w_sem.at[part]) for part in range(3)
     ]
     for copy in w_copies:
         copy.start()
 
-    sent = [1]
-
-    def send_patch(slot, seq, mp):
-        push(
-            patch_buf.at[slot, c],
-            patch_buf.at[slot, c],
-            patch_send.at[sent[0]],
-            patch_recv.at[slot, c],
-            seq,
-            mp,
-        )
-        sent[0] += 1
+    def forward_patch(slot, seq, mp):
+        pair = patch_buf.at[slot, c]
+        send_patch(pair, pair, patch_recv.at[slot, c], seq, mp)
 
     def wait_patch(slot, core):
         arrived(patch_buf.at[slot, core], patch_send.at[0], patch_recv.at[slot, core])
 
-    arrived(patch_buf.at[s, c, 1 - x], patch_send.at[0], far_recv.at[0])
-    for step in range(1, groups):
-        send_patch(s, (g + step) % groups * ranks + r, m)
     for group_step in range(groups):
-        slot = (g + group_step) % groups * ranks + r
+        slot = (g + groups - group_step) % groups * ranks + r
         if group_step:
-            wait_patch(slot, c)
+            arrived(patch_buf.at[slot, c, x], patch_send.at[0], half_recv.at[slot, x])
+        arrived(patch_buf.at[slot, c, 1 - x], patch_send.at[0], half_recv.at[slot, 1 - x])
         for step in range(1, ranks):
-            send_patch(slot, g * ranks + (r + step) % ranks, m)
-        send_patch(slot, s, near)
-        if group_step == 0:
-            push(text_ref, text_buf.at[m], text_send.at[0], text_recv.at[m], s, far)
-            push(text_ref, text_buf.at[m], text_send.at[1], text_recv.at[m], s, near)
+            forward_patch(slot, g * ranks + (r + step) % ranks, m)
+        forward_patch(slot, s, near)
     for group_step in range(groups):
         for step in range(1, ranks):
-            slot = (g + group_step) % groups * ranks + (r + step) % ranks
+            slot = (g + groups - group_step) % groups * ranks + (r + step) % ranks
             wait_patch(slot, c)
-            send_patch(slot, s, near)
+            forward_patch(slot, s, near)
 
     loads[2].wait()
     for peer in (far, near_far, near):
@@ -646,7 +649,7 @@
     dma = pltpu.SemaphoreType.DMA
     return pl.pallas_call(
         functools.partial(fused_kernel, n_s, n_m, groups),
-        out_shape=jax.ShapeDtypeStruct((tok_rows, groups * HD), bf16),
+        out_shape=pltpu.VMEM((tok_rows, groups * HD), bf16),
         in_specs=[
             pl.BlockSpec(memory_space=pltpu.SMEM),
             hbm,
@@ -683,8 +686,8 @@
             dma((n_m,)),
             dma((3,)),
             dma((n_m,)),
-            dma((1 + groups - 1 + groups * (ranks - 1) + n_s,)),
-            dma((1,)),
+            dma((1 + 2 * (groups - 1) + groups * (ranks - 1) + n_s,)),
+            dma((n_s, 2)),
             dma((n_s, 2)),
             dma((n_s - 1 + 2 * n_s,)),
             dma((n_s, 2)),

time: 59.5 us -> 56.3 us (0.946)
  Pallas kernels: 57.7 us -> 55.5 us
  local copies, waits for them, and re-layouts: 1.57 us -> 0.66 us
    pallas_call x1, Pallas kernels: 57.7 us -> 55.5 us  [fused_shards(): pl.pallas_call(functools.partial(fused_kernel, n_s, n_m, groups), out_sha...]
    unnamed x1, local copies, waits for them, and re-layouts: 1.57 us -> 0.66 us
where the time goes in v4:
time: 56.3 us; the launch traced here: 56.1 us
  Pallas kernels  55.5 us (99%)
  local copies, waits for them, and re-layouts  0.66 us (1%)
    pallas_call x1, Pallas kernels, fused_shards(): pl.pallas_call(functools.partial(fused_kernel, n_s, n_m, groups), out_sha...  55.5 us

profile of v4, /device:TPU:0, one launch (start us, length us, event | category | flops | bytes accessed | tf_op | source)
XLA Modules:
  0.0 56.1 jit_solution(12449234026402367043)
XLA Ops:
  0.0 55.5 %shard_map.64 = bf16[128,512]{1,0:T(8,128)(2,1)S(1)} custom-call(s32[1024]{0:T(1024)} %seg_ref.1, bf16[2,128,256]{2,1,0:T(8,128)(2,1)} %lat_ref.1, bf16[3,3,64,256]{3,2,1,0:T(8,128)(2,1)} %bitcast.4, bf16[256,512]{1,0:T(8,128)(2,1)} %bitcast.5, bf16[128,1024]{1,0:T(8,128)(2,1)} %text_ref.1, bf16[3,4096,512]{2,1,0:T(8,128)(2,1)} %bitcast.3), custom_call_target="tpu_custom_call" | custom-call | flops 1610612736 | bytes 12582912 | tf_op jit(solution)/shard_map/pallas_call | solution.py:650
  55.5 0.7 %copy.8 = bf16[128,512]{1,0:T(8,128)(2,1)} copy(bf16[128,512]{1,0:T(8,128)(2,1)S(1)} %shard_map.64) | data formatting | bytes 262144

commit v5 on v4

--- a/solution.py
+++ b/solution.py
@@ -178,6 +178,7 @@
     emb_pad,
     emb_out,
     hid_buf,
+    hid_rows,
     acc,
     qkv_out,
     qkv_buf,
@@ -461,6 +462,9 @@
             m,
         )
     put_block(hid_buf.at[s, c, x], s)
+    loads[3].wait()
+    arrived(text_buf.at[far], text_send.at[0], text_recv.at[far])
+    push(text_buf.at[far], text_buf.at[far], text_send.at[2], text_recv.at[far], s, near)
     for step in range(n_s):
         slot = (s + n_s - step) % n_s
         if step:
@@ -473,9 +477,6 @@
             s,
             far,
         )
-    loads[3].wait()
-    arrived(text_buf.at[far], text_send.at[0], text_recv.at[far])
-    push(text_buf.at[far], text_buf.at[far], text_send.at[2], text_recv.at[far], s, near)
     for step in range(n_s):
         slot = (s + n_s - step) % n_s
         arrived(hid_buf.at[slot, c, 1 - x], hid_send.at[0], hid_recv.at[slot, 1 - x])
@@ -495,6 +496,18 @@
     is_image = (my_pos >= start) & (my_pos < start + img_toks)
     per_text = text_ref.shape[1] // width
     deep = 2 * width
+
+    def project(part, slot, hidden, first):
+        product = jnp.dot(
+            hidden,
+            w_buf[part, pl.ds(pl.multiple_of(slot * deep, deep), deep)],
+            preferred_element_type=jnp.float32,
+        )
+        if first:
+            acc[part] = product
+        else:
+            acc[part] += product
+
     for step in range(n_s):
         slot = (s + n_s - step) % n_s
         arrived(hid_buf.at[slot, 1 - c], hid_send.at[0], near_recv.at[slot])
@@ -512,22 +525,14 @@
             )
             pieces.append(jnp.where(is_image, image, text))
         hidden = jnp.concatenate(pieces, axis=1)
-        for part in range(3):
-            product = jnp.dot(
-                hidden,
-                w_buf[part, pl.ds(pl.multiple_of(slot * deep, deep), deep)],
-                preferred_element_type=jnp.float32,
-            )
-            if step == 0:
-                acc[part] = product
-            else:
-                acc[part] += product
-
-    for head in range(groups):
-        for part in range(3):
-            qkv_out[head, :, part * HD : (part + 1) * HD] = acc[
-                part, :, head * HD : (head + 1) * HD
-            ].astype(jnp.bfloat16)
+        hid_rows[slot] = hidden
+        for part in range(1, 3):
+            project(part, slot, hidden, step == 0)
+
+    def cast_head(head, part):
+        at = pl.ds(pl.multiple_of(head * HD, HD), HD)
+        qkv_out[head, :, part * HD : (part + 1) * HD] = acc[part, :, at].astype(jnp.bfloat16)
+
     sent_qkv = [0]
 
     def send_qkv(src, dst, slot, seq):
@@ -538,15 +543,24 @@
     query_cols = pl.ds(0, HD)
     for step in range(1, groups):
         head = (g + step) % groups
+        cast_head(head, 1)
+        cast_head(head, 2)
         send_qkv(
             qkv_out.at[head, :, key_cols], qkv_buf.at[s, :, key_cols], s, head * ranks + r
         )
-    qkv_buf[s] = qkv_out[g]
+    cast_head(g, 1)
+    cast_head(g, 2)
+    qkv_buf[s, :, key_cols] = qkv_out[g, :, key_cols]
     for step in range(1, ranks):
         kv = qkv_buf.at[s, :, key_cols]
         send_qkv(kv, kv, s, g * ranks + (r + step) % ranks)
+    for slot in range(n_s):
+        project(0, slot, hid_rows[slot], slot == 0)
+    cast_head(g, 0)
+    qkv_buf[s, :, query_cols] = qkv_out[g, :, query_cols]
     for step in range(1, groups):
         head = (g + step) % groups
+        cast_head(head, 0)
         push(
             qkv_out.at[head, :, query_cols],
             qkv_buf.at[s, :, query_cols],
@@ -671,6 +685,7 @@
             pltpu.VMEM(((2 * total_len - img_toks) // half, half // 2, width), bf16),
             pltpu.VMEM((n_s, tok_rows // half, half // 2, width), bf16),
             pltpu.VMEM((n_s, 2, 2, tok_rows // half, half // 2, width), bf16),
+            pltpu.VMEM((n_s, tok_rows, 2 * width), bf16),
             pltpu.VMEM((3, tok_rows, wqkv.shape[2]), jnp.float32),
             pltpu.VMEM((groups, tok_rows, 3 * HD), bf16),
             pltpu.VMEM((n_s, tok_rows, 3 * HD), bf16),

time: 56.3 us -> 54.2 us (0.963)
  Pallas kernels: 55.5 us -> 53.3 us
    pallas_call x1, Pallas kernels: 55.5 us -> 53.3 us  [fused_shards(): pl.pallas_call(functools.partial(fused_kernel, n_s, n_m, groups), out_sha...]
where the time goes in v5:
time: 54.2 us; the launch traced here: 54 us
  Pallas kernels  53.3 us (98%)
  local copies, waits for them, and re-layouts  0.66 us (1%)
    pallas_call x1, Pallas kernels, fused_shards(): pl.pallas_call(functools.partial(fused_kernel, n_s, n_m, groups), out_sha...  53.3 us

profile of v5, /device:TPU:0, one launch (start us, length us, event | category | flops | bytes accessed | tf_op | source)
XLA Modules:
  0.0 54.0 jit_solution(1828402475225862987)
XLA Ops:
  0.0 53.3 %shard_map.64 = bf16[128,512]{1,0:T(8,128)(2,1)S(1)} custom-call(s32[1024]{0:T(1024)} %seg_ref.1, bf16[2,128,256]{2,1,0:T(8,128)(2,1)} %lat_ref.1, bf16[3,3,64,256]{3,2,1,0:T(8,128)(2,1)} %bitcast.4, bf16[256,512]{1,0:T(8,128)(2,1)} %bitcast.5, bf16[128,1024]{1,0:T(8,128)(2,1)} %text_ref.1, bf16[3,4096,512]{2,1,0:T(8,128)(2,1)} %bitcast.3), custom_call_target="tpu_custom_call" | custom-call | flops 1610612736 | bytes 12582912 | tf_op jit(solution)/shard_map/pallas_call | solution.py:664
  53.3 0.7 %copy.8 = bf16[128,512]{1,0:T(8,128)(2,1)} copy(bf16[128,512]{1,0:T(8,128)(2,1)S(1)} %shard_map.64) | data formatting | bytes 262144

commit v6 on v5

--- a/solution.py
+++ b/solution.py
@@ -477,7 +477,7 @@
             s,
             far,
         )
-    for step in range(n_s):
+    def to_near(step):
         slot = (s + n_s - step) % n_s
         arrived(hid_buf.at[slot, c, 1 - x], hid_send.at[0], hid_recv.at[slot, 1 - x])
         push(
@@ -488,6 +488,10 @@
             s,
             near,
         )
+
+    late = 2
+    for step in range(n_s - late):
+        to_near(step)
     arrived(text_buf.at[near], text_send.at[0], text_recv.at[near])
     arrived(text_buf.at[near_far], text_send.at[0], text_recv.at[near_far])
     for copy in w_copies:
@@ -528,6 +532,8 @@
         hid_rows[slot] = hidden
         for part in range(1, 3):
             project(part, slot, hidden, step == 0)
+        if step < late:
+            to_near(n_s - late + step)
 
     def cast_head(head, part):
         at = pl.ds(pl.multiple_of(head * HD, HD), HD)

time: 54.2 us -> 53.9 us (level)
  no operation moved by 1% of the time
where the time goes in v6:
time: 53.9 us; the launch traced here: 53.7 us
  Pallas kernels  53 us (98%)
  local copies, waits for them, and re-layouts  0.66 us (1%)
    pallas_call x1, Pallas kernels, fused_shards(): pl.pallas_call(functools.partial(fused_kernel, n_s, n_m, groups), out_sha...  53 us

profile of v6, /device:TPU:0, one launch (start us, length us, event | category | flops | bytes accessed | tf_op | source)
XLA Modules:
  0.0 53.7 jit_solution(2334543089037737742)
XLA Ops:
  0.0 53.0 %shard_map.64 = bf16[128,512]{1,0:T(8,128)(2,1)S(1)} custom-call(s32[1024]{0:T(1024)} %seg_ref.1, bf16[2,128,256]{2,1,0:T(8,128)(2,1)} %lat_ref.1, bf16[3,3,64,256]{3,2,1,0:T(8,128)(2,1)} %bitcast.4, bf16[256,512]{1,0:T(8,128)(2,1)} %bitcast.5, bf16[128,1024]{1,0:T(8,128)(2,1)} %text_ref.1, bf16[3,4096,512]{2,1,0:T(8,128)(2,1)} %bitcast.3), custom_call_target="tpu_custom_call" | custom-call | flops 1610612736 | bytes 12582912 | tf_op jit(solution)/shard_map/pallas_call | solution.py:670
  53.0 0.7 %copy.8 = bf16[128,512]{1,0:T(8,128)(2,1)} copy(bf16[128,512]{1,0:T(8,128)(2,1)S(1)} %shard_map.64) | data formatting | bytes 262144
